TPU v7x, 32 devices: a whole 2x2x4 slice. The times are simulated.
32 devices in a mesh: groups: 2 (over y), row: 8 (over z, x), col: 2 (over core).
Axes of the slice: x: 2, y: 2, z: 4, core: 2. Of those that a mesh axis runs over, the one named last changes fastest.
Arguments:
- gram_old: bfloat16 [28672, 14336], P(('groups', 'row'), 'col'), parts along dimension 0, may hold values from -10 to 256, as said below
- activations: bfloat16 [256, 14336], P('groups', 'row'), parts along dimension 0, may hold values from -0.5 to 0.5
- weights: float32 [14336, 512], P('row', ('groups', 'col')), parts along dimension 1, may hold values from -6 to 6
- block_mask: int32 [112, 4], P(None, 'groups'), parts along dimension 1, may hold values 0 or 1
Outputs:
- pruned: float32 [14336, 512], P('row', ('groups', 'col')), parts along dimension 1
There are 2 independent parts, one for each index of `groups`. A program takes and returns all parts, laid end to end along the dimension named above; each array names one. Nothing has to cross between parts.
Inputs may be any that keep to these rules, and one draw needn't show every extreme that they name: `gram_old`: symmetric and positive definite.
All inputs are finite; a program needn't handle non-finite values.
Results may differ from a plain program's by a relative error of at most 0.00076.
Values may be sent and summed in bfloat16 or wider, within the bound.
No kernel may reach another device: no remote copies, remote signals or barrier semaphores. Data moves between devices by JAX's collectives and lax.ppermute only.
A program may use at most 128 MiB of HBM per device.

v0:
```python
import functools

import jax
import jax.numpy as jnp
from jax import lax
from jax.experimental import pallas as pl
from jax.experimental.pallas import tpu as pltpu
from jax.sharding import PartitionSpec as P

BLK = 128
TILE = 896
PART = 448
LIMIT = 8 * 1024 * 1024
AXES = ("row", "col")

damping_ratio = 0.3
epsilon = 1e-06


def swap(value, axis, distance):
    return lax.ppermute(value, axis, [(i, i ^ distance) for i in range(lax.axis_size(axis))])


def sum_part(value, count):
    devices = 2 * count
    shifts = [[(i, i ^ k) for i in range(devices)] for k in (1, 2, 3)]
    value += sum(lax.ppermute(value, AXES, pairs) for pairs in shifts)
    shifts = [[(i, (i + k) % devices) for i in range(devices)] for k in range(4, devices, 4)]
    return value + sum(lax.ppermute(value, AXES, pairs) for pairs in shifts)


def expand_local(block_mask, row_index, row_block, col_index, width_cols):
    if width_cols != BLK:
        row_ids = (row_index * row_block + jnp.arange(row_block, dtype=jnp.int32)) // BLK
        col_ids = (col_index * width_cols + jnp.arange(width_cols, dtype=jnp.int32)) // BLK
        return block_mask[row_ids][:, col_ids].astype(jnp.float32)
    piece = BLK
    while row_block % piece:
        piece //= 2
    column = lax.dynamic_index_in_dim(block_mask, col_index, 1, keepdims=False)
    column = jnp.repeat(column, BLK // piece) if piece != BLK else column
    count = row_block // piece
    own = lax.dynamic_slice_in_dim(column, row_index * count, count, 0).astype(jnp.float32)
    return jnp.broadcast_to(own[:, None, None], (count, piece, width_cols)).reshape(
        row_block, width_cols
    )


class Ring:
    def __init__(self, count):
        self.count = count
        self.order = list(range(0, count, 2)) + list(range(count - 1, 0, -2))
        self.last = count // 2 - 1

    def row(self, place):
        return self.order[place % self.count]

    def half(self, place):
        return self.row(place) * 2 // self.count

    def ahead(self, place):
        return int(place % self.count >= self.count // 2)

    def device(self, place, core):
        return self.row(place) * 2 + core

    def source(self, place, core, step):
        return place - 1 - step if core == self.ahead(place) else place + 1 + step

    def first_column(self, place, core, step):
        origin = self.ahead(self.source(place, core, step))
        return origin if core == self.ahead(place) else 1 - origin

    def places(self):
        return [(place, core) for place in range(self.count) for core in range(2)]

    def shift(self):
        pairs = []
        for place in range(self.count):
            pairs.append(
                (self.device(place, self.ahead(place)), self.device(place + 1, self.ahead(place + 1)))
            )
            pairs.append(
                (
                    self.device(place, 1 - self.ahead(place)),
                    self.device(place - 1, 1 - self.ahead(place - 1)),
                )
            )
        return pairs

    def hand_over(self, step):
        return [
            (self.device(place, core), self.device(place, 1 - core))
            for place, core in self.places()
            if self.half(self.source(place, core, step)) != core
        ]

    def slots(self):
        found = []
        for step in range(self.last):
            found.append((True, step))
            if self.hand_over(step):
                found.append((False, step))
        return found + [(True, self.last)]

    def loads(self, slot):
        base = 3 * (1 + len(self.slots()))
        return [base + slot + 1] if slot + 1 < self.count // 2 else []

    def entry(self, place, core, carrier, step):
        source = self.source(place, carrier, step)
        return [
            self.row(source) % (self.count // 2),
            int(self.half(source) == core),
            int(self.first_column(place, carrier, step) != core),
        ]

    def table(self):
        half = self.count // 2
        lines = [None] * (2 * self.count)
        for place, core in self.places():
            line = [self.row(place) % half, int(self.half(place) == core), 0]
            for carrier, step in self.slots():
                line += self.entry(place, core, core if carrier else 1 - core, step)
            needed = [line[k] for k in range(0, len(line), 3) if line[k + 1]]
            line += needed
            lines[self.device(place, core)] = line
        return lines


def pick(ring, entry):
    device = lax.axis_index("row") * 2 + lax.axis_index("col")
    values = [line[entry] for line in ring.table()]
    picked = jnp.int32(values[0])
    for index, value in enumerate(values):
        if value != values[0]:
            picked = jnp.where(device == index, jnp.int32(value), picked)
    return picked


def block_copies(ring, load, gram, store, sems):
    rows = gram.shape[0]
    there = pl.ds(pl.multiple_of(pick(ring, load) * rows, BLK), rows)
    parts = [pl.ds(part * PART, PART) for part in range(rows // PART)]
    return [
        pltpu.make_async_copy(gram.at[here, there], store.at[here, there], sems.at[part])
        for part, here in enumerate(parts)
    ]


def load_kernel(ring, load, gram, acts, second, store, across, passed, sems):
    copies = block_copies(ring, load, gram, store, sems)
    for copy in copies:
        copy.start()
    across[...] = acts[...].astype(jnp.float32).T.astype(across.dtype)
    for copy in copies:
        copy.wait()


def load_first(ring, gram, acts, second):
    whole = pl.BlockSpec(memory_space=pltpu.VMEM)
    return pl.pallas_call(
        functools.partial(load_kernel, ring, ring.loads(-1)[0]),
        in_specs=[pl.BlockSpec(memory_space=pltpu.HBM), whole, whole],
        out_specs=[whole] * 3,
        out_shape=[
            jax.ShapeDtypeStruct(gram.shape, gram.dtype),
            jax.ShapeDtypeStruct(acts.shape[::-1], acts.dtype),
            jax.ShapeDtypeStruct(second.shape, second.dtype),
        ],
        scratch_shapes=[pltpu.SemaphoreType.DMA((gram.shape[0] // PART,))],
        input_output_aliases={2: 2},
        compiler_params=pltpu.CompilerParams(vmem_limit_bytes=LIMIT),
    )(gram, acts, second)


def product_kernel(ring, slot, loads, with_trace, first, second, across, *refs):
    copies = []
    if with_trace:
        acts, gram, _, own, other, store, trace, sems = refs
        trace[...] = jnp.zeros_like(trace)
    elif loads:
        gram, _, own, other, store, sems = refs[-6:]
    else:
        own, other, store = refs[-3:]
    if loads:
        copies = block_copies(ring, loads[0], gram, store, sems)
    for copy in copies:
        copy.start()
    rows, width = own.shape
    start = pl.multiple_of(pick(ring, 3 * slot) * rows, BLK)
    flip = pick(ring, 3 * slot + 2) == 1
    if slot == 0:
        own[...] = jnp.zeros_like(own)
        other[...] = jnp.zeros_like(other)

    @pl.when(pick(ring, 3 * slot + 1) == 1)
    def _():
        @pl.loop(0, rows // TILE)
        def _(tile):
            here = pl.ds(pl.multiple_of(tile * TILE, TILE), TILE)
            lines = jnp.concatenate([store[here, pl.ds(start, rows)], across[here, :]], axis=1)
            panel = jnp.concatenate([first[...], second[...]], axis=1)
            result = jnp.dot(lines, panel, preferred_element_type=jnp.float32)
            left, right = result[:, :width], result[:, width:]
            own[here, :] += jnp.where(flip, right, left)
            other[here, :] += jnp.where(flip, left, right)

        if with_trace:
            add_diagonal(store, start, acts, trace)

    for copy in copies:
        copy.wait()


def add_diagonal(store, start, acts, trace):
    lines = lax.broadcasted_iota(jnp.int32, (BLK, BLK), 0)
    same = lines == lax.broadcasted_iota(jnp.int32, (BLK, BLK), 1)
    for block in range(acts.shape[1] // BLK):
        here = slice(block * BLK, (block + 1) * BLK)
        there = pl.ds(pl.multiple_of(start + block * BLK, BLK), BLK)
        square = store[here, there].astype(jnp.float32)
        diag = jnp.sum(jnp.where(same, square, 0.0), axis=0, keepdims=True)
        part = acts[:, here].astype(jnp.float32)
        diag += jnp.sum(part * part, axis=0, keepdims=True)
        trace[0:1, :] += diag.astype(jnp.bfloat16).astype(jnp.float32)


def product(ring, slot, loads, gram, store, message, across, acts, acc):
    rows = across.shape[0]
    width = message[0].shape[1]
    whole = pl.BlockSpec(memory_space=pltpu.VMEM)
    with_trace = bool(loads) and slot == 0
    operands = [*message, across]
    aliases = {len(operands) + k: k for k in range(len(acc))}
    operands += acc
    in_specs = [whole] * (len(operands) + 1)
    out_shape = [jax.ShapeDtypeStruct((rows, width), jnp.float32)] * 2
    out_shape.append(jax.ShapeDtypeStruct(store.shape, store.dtype))
    scratch = []
    if with_trace:
        operands.append(acts)
        in_specs.append(whole)
        out_shape.append(jax.ShapeDtypeStruct((8, width), jnp.float32))
    aliases[len(operands) + bool(loads)] = 2
    if loads:
        operands.append(gram)
        in_specs.insert(len(operands) - 1, pl.BlockSpec(memory_space=pltpu.HBM))
        scratch = [pltpu.SemaphoreType.DMA((rows // PART,))]
    operands.append(store)
    results = pl.pallas_call(
        functools.partial(product_kernel, ring, slot, loads, with_trace),
        in_specs=in_specs,
        out_specs=[whole] * len(out_shape),
        out_shape=out_shape,
        scratch_shapes=scratch,
        input_output_aliases=aliases,
        compiler_params=pltpu.CompilerParams(vmem_limit_bytes=LIMIT),
        cost_estimate=pl.CostEstimate(
            flops=4 * rows * rows * width, bytes_accessed=2 * rows * rows, transcendentals=0
        ),
    )(*operands)
    return results[:2], results[2], results[3:]


def after(value, others):
    return lax.optimization_barrier((value, *others))[0]


def ring_apply(ring, gram, message, acts, early):
    first = message
    trace = []
    store, across, second = early(swap(message, "col", 1))
    ready = [(first, second)]
    acc = []
    slot = 0

    def work(others=()):
        nonlocal acc, store, slot, trace
        if not ready:
            return
        parts = ready.pop(0)
        parts = (after(parts[0], others), parts[1])
        loads = [] if gram is None else ring.loads(slot)
        acc, store, added = product(ring, slot, loads, gram, store, parts, across, acts, acc)
        trace = trace or added
        slot += 1

    def hand_over(step):
        if ring.hand_over(step):
            ready.append(tuple(swap(after(part, acc[:1]), "col", 1) for part in held))

    for step in range(ring.last):
        came = lax.ppermute(after(first, acc[:1]), AXES, ring.shift())
        if step:
            work([first])
        second = lax.ppermute(after(second, acc[:1]), AXES, ring.shift())
        if step:
            hand_over(step - 1)
            work()
        first = came
        held = (first, second)
        ready.append(held)
    first = lax.ppermute(after(first, acc[:1]), AXES, ring.shift())
    hand_over(ring.last - 1)
    work()
    last = (first, swap(after(first, acc[:1]), "col", 1))
    while ready:
        work()
    ready.append(last)
    work()
    return acc[0], swap(acc[1], "col", 1), store, trace


def put_message(message, acts, rows):
    message[rows:, :] = jnp.dot(
        acts[...], message[:rows, :], preferred_element_type=jnp.float32
    ).astype(message.dtype)


def head_kernel(weights, blocks, acts, message):
    rows = weights.shape[0]
    for block in range(rows // BLK):
        here = slice(block * BLK, (block + 1) * BLK)
        dense = weights[here, :]
        message[here, :] = (blocks[block : block + 1, :] * dense - dense).astype(message.dtype)
    put_message(message, acts, rows)


def turn_kernel(own, received, blocks, acts, _, grad, message, __):
    rows = own.shape[0]
    for block in range(rows // BLK):
        here = slice(block * BLK, (block + 1) * BLK)
        grad_first = own[here, :] + received[here, :]
        grad[here, :] = grad_first
        message[here, :] = (blocks[block : block + 1, :] * grad_first).astype(message.dtype)
    put_message(message, acts, rows)


def lane_sums(value):
    return jnp.sum(value, axis=0, keepdims=True)


def curve_kernel(trace, grad, own, received, blocks, curve_ref, sums_ref):
    rows = grad.shape[0]
    sums_ref[...] = jnp.zeros_like(sums_ref)
    sums_ref[0:1, :] = trace[0:1, :]
    for block in range(rows // BLK):
        here = slice(block * BLK, (block + 1) * BLK)
        kept = blocks[block : block + 1, :]
        curve = own[here, :] + received[here, :]
        curve_ref[here, :] = curve
        step_dir = kept * grad[here, :]
        masked = kept * curve
        sums_ref[1:2, :] += lane_sums(step_dir * step_dir)
        sums_ref[2:3, :] += lane_sums(step_dir * curve)
        sums_ref[3:4, :] += lane_sums(masked * masked)


def last_kernel(units, sums, grad, curve, weights, blocks, out_ref):
    totals = jnp.sum(sums[...], axis=1, keepdims=True)
    trace_total, grad_square = totals[0:1, :], totals[1:2, :]
    grad_curve, curve_square = totals[2:3, :], totals[3:4, :]
    damping = damping_ratio * trace_total / units
    step_first = grad_square / (grad_curve + damping * grad_square + epsilon)
    step_second = (grad_curve + damping * grad_square) / (
        curve_square + 2.0 * damping * grad_curve + damping * damping * grad_square + epsilon
    )
    rows = grad.shape[0]
    for block in range(rows // BLK):
        here = slice(block * BLK, (block + 1) * BLK)
        kept = blocks[block : block + 1, :]
        grad_first = grad[here, :]
        step_dir = kept * grad_first
        grad_second = grad_first - step_first * curve[here, :]
        out_ref[here, :] = (
            kept * weights[here, :] - step_first * step_dir - step_second * (kept * grad_second)
        )


def gather_apply(gram, activations, panel, col_index):
    half = gram.shape[1]
    full = lax.all_gather(panel, "row", axis=0, tiled=True)
    own_half = lax.dynamic_slice_in_dim(full, col_index * half, half, 0)
    need = lax.dynamic_slice_in_dim(full, (1 - col_index) * half, half, 0)
    other_half = swap(need, "col", 1)
    own = jnp.dot(gram, own_half, preferred_element_type=jnp.float32)
    partial = jnp.dot(gram, other_half, preferred_element_type=jnp.float32)
    low = lax.psum(jnp.dot(activations, panel, preferred_element_type=jnp.float32), "row")
    update = lax.dot_general(
        activations.astype(jnp.float32),
        low,
        (((0,), (0,)), ((), ())),
        precision=lax.Precision.HIGHEST,
        preferred_element_type=jnp.float32,
    )
    return own + swap(partial, "col", 1) + update


def per_device_general(gram_old, activations, weights, block_mask):
    row_block, half_width = gram_old.shape
    width_cols = weights.shape[1]
    units = lax.axis_size("row") * row_block
    row_index = lax.axis_index("row")
    col_index = lax.axis_index("col")
    mask_local = expand_local(block_mask, row_index, row_block, col_index, width_cols)
    kept_weights = mask_local * weights
    diff_low = (kept_weights - weights).astype(jnp.bfloat16)
    acts = activations.astype(jnp.float32)
    column_squares = jnp.sum(acts * acts, axis=0)
    grad_first = gather_apply(gram_old, activations, diff_low, col_index)
    place = row_index * row_block + jnp.arange(row_block, dtype=jnp.int32)
    place = place - col_index * half_width
    on_diagonal = jnp.arange(half_width, dtype=jnp.int32)[None, :] == place[:, None]
    new_gram = gram_old.astype(jnp.float32) + column_squares[:, None]
    new_gram = new_gram.astype(jnp.bfloat16).astype(jnp.float32)
    trace_part = jnp.sum(jnp.where(on_diagonal, new_gram, 0.0))
    step_dir = mask_local * grad_first
    curvature = gather_apply(gram_old, activations, step_dir.astype(jnp.bfloat16), col_index)
    masked_curve = mask_local * curvature
    sums = jnp.stack(
        [
            trace_part,
            jnp.sum(step_dir * step_dir),
            jnp.sum(step_dir * curvature),
            jnp.sum(masked_curve * masked_curve),
        ]
    )
    sums = lax.psum(sums, ("row", "col"))
    trace_total, grad_square, grad_curve, curve_square = sums[0], sums[1], sums[2], sums[3]
    damping = damping_ratio * trace_total / units
    step_first = grad_square / (grad_curve + damping * grad_square + epsilon)
    step_second = (grad_curve + damping * grad_square) / (
        curve_square + 2.0 * damping * grad_curve + damping * damping * grad_square + epsilon
    )
    grad_second = grad_first - step_first * curvature
    return kept_weights - step_first * step_dir - step_second * (mask_local * grad_second)


def call_whole(kernel, out_shape, *operands, alias={}):
    whole = pl.BlockSpec(memory_space=pltpu.VMEM)
    return pl.pallas_call(
        kernel,
        in_specs=[whole] * len(operands),
        out_specs=[whole] * len(out_shape),
        out_shape=out_shape,
        input_output_aliases=alias,
        compiler_params=pltpu.CompilerParams(vmem_limit_bytes=LIMIT),
    )(*operands)


def per_device(gram_old, activations, weights, block_mask):
    row_block, _ = gram_old.shape
    width = weights.shape[1]
    samples = activations.shape[0]
    count = lax.axis_size("row")
    if row_block % TILE or count not in (4, 8, 16) or width != BLK or samples % 16:
        return per_device_general(gram_old, activations, weights, block_mask)
    ring = Ring(count)
    row_index = lax.axis_index("row")
    col_index = lax.axis_index("col")
    per_block = row_block // BLK
    own_mask = lax.dynamic_slice(block_mask, (row_index * per_block, col_index), (per_block, 1))
    blocks = jnp.broadcast_to(own_mask.astype(jnp.float32), (per_block, width))
    panel = jax.ShapeDtypeStruct((row_block, width), jnp.float32)
    letter = jax.ShapeDtypeStruct((row_block + samples, width), jnp.bfloat16)
    eight = jax.ShapeDtypeStruct((8, width), jnp.float32)

    (message,) = call_whole(head_kernel, [letter], weights, blocks, activations)
    across = None

    def load(second):
        nonlocal across
        store, across, second = load_first(ring, gram_old, activations, second)
        return store, across, second

    own, received, store, (trace,) = ring_apply(ring, gram_old, message, activations, load)
    held = jax.ShapeDtypeStruct(store.shape, store.dtype)
    grad, message, store = call_whole(
        turn_kernel, [panel, letter, held], own, received, blocks, activations, store, alias={4: 2}
    )

    def keep(second):
        return store, across, second

    own, received, _, _ = ring_apply(ring, None, message, activations, keep)
    curve, sums = call_whole(curve_kernel, [panel, eight], trace, grad, own, received, blocks)
    sums = sum_part(sums, count)
    last = functools.partial(last_kernel, float(count * row_block))
    return call_whole(last, [panel], sums, grad, curve, weights, blocks)[0]


def solution(mesh):
    placed = (
        P(("groups", "row"), "col"),
        P("groups", "row"),
        P("row", ("groups", "col")),
        P(None, "groups"),
    )
    return jax.shard_map(
        per_device,
        mesh=mesh,
        in_specs=placed,
        out_specs=P("row", ("groups", "col")),
        check_vma=False,
    )
```

profile of v0, /device:TPU:0, one launch (start us, length us, event | category | flops | bytes accessed | tf_op | source)
XLA Modules:
  0.0 117.4 jit_solution(5059932368146477528)
XLA Ops:
  3.9 2.6 %collective-permute-start = (bf16[1920,128]{1,0:T(8,128)(2,1)S(1)}, bf16[1920,128]{1,0:T(8,128)(2,1)S(1)}, u32[]{:S(2)}, u32[]{:S(2)}) collective-permute-start(bf16[1920,128]{1,0:T(8,128)(2,1)S(1)} %shard_map.46.first), channel_id=1, source_target_pairs={{0,4},{1,2},{4,8},{5,1},{8,12},{9,5},{12,15},{13,9},{15,11},{14,13... | collective-permute-start | bytes 1474568 | tf_op jit(solution)/shard_map/ppermute | solution.py:294
  7.5 3.0 %shard_map.47 = (bf16[1792,7168]{1,0:T(8,128)(2,1)S(1)}, bf16[1792,128]{1,0:T(8,128)(2,1)S(1)}, bf16[1920,128]{1,0:T(8,128)(2,1)S(1)}) custom-call(bf16[1792,7168]{1,0:T(8,128)(2,1)} %refs_2_.3, bf16[128,1792]{1,0:T(8,128)(2,1)S(1)} %copy-done.1, bf16[1920,128]{1,0:T(8,128)(2,1)S(1)} %collective-permute-done.1.second), custom_call_target="tpu_custom_call", output_to_operand_aliasing={{2}: (2, {})} | custom-call | tf_op jit(solution)/shard_map/pallas_call | solution.py:162
  13.0 2.4 %collective-permute-start.2 = (bf16[1920,128]{1,0:T(8,128)(2,1)S(1)}, bf16[1920,128]{1,0:T(8,128)(2,1)S(1)}, u32[]{:S(2)}, u32[]{:S(2)}) collective-permute-start(bf16[1920,128]{1,0:T(8,128)(2,1)S(1)} %collective-permute-done.first), channel_id=1, source_target_pairs={{0,4},{1,2},{4,8},{5,1},{8,12},{9,5},{12,15},{13,9},{15,11},{14,13... | collective-permute-start | bytes 1474568 | tf_op jit(solution)/shard_map/ppermute | solution.py:294
  15.4 3.0 %shard_map.48 = (f32[1792,128]{1,0:T(8,128)S(1)}, f32[1792,128]{1,0:T(8,128)S(1)}, bf16[1792,7168]{1,0:T(8,128)(2,1)S(1)}, f32[8,128]{1,0:T(8,128)S(1)}) custom-call(bf16[1920,128]{1,0:T(8,128)(2,1)S(1)} %shard_map.46.first, bf16[1920,128]{1,0:T(8,128)(2,1)S(1)} %get-tuple-element.74.second, ...), custom_call_target="tpu_custom_call", output_to_operand_aliasing={{2}: (5, {})} | custom-call | flops 1644167168 | bytes 6422528 | tf_op jit(solution)/shard_map/pallas_call | solution.py:251
  21.2 2.9 %shard_map.49 = (f32[1792,128]{1,0:T(8,128)S(1)}, f32[1792,128]{1,0:T(8,128)S(1)}, bf16[1792,7168]{1,0:T(8,128)(2,1)S(1)}) custom-call(bf16[1920,128]{1,0:T(8,128)(2,1)S(1)} %collective-permute-done.first, bf16[1920,128]{1,0:T(8,128)(2,1)S(1)} %collective-permute-done.3.second, ...), custom_call_target="tpu_custom_call", output_to_operand_aliasing={{0}: (3, {}), {1}: (4, {}), {2}: (6, {})} | custom-call | flops 1644167168 | bytes 6422528 | tf_op jit(solution)/shard_map/pallas_call | solution.py:251
  24.1 2.3 %collective-permute-start.4 = (bf16[1920,128]{1,0:T(8,128)(2,1)S(1)}, bf16[1920,128]{1,0:T(8,128)(2,1)S(1)}, u32[]{:S(2)}, u32[]{:S(2)}) collective-permute-start(bf16[1920,128]{1,0:T(8,128)(2,1)S(1)} %collective-permute-done.2.first), channel_id=1, source_target_pairs={{0,4},{1,2},{4,8},{5,1},{8,12},{9,5},{12,15},{13,9},{15,11},{14,13... | collective-permute-start | bytes 1474568 | tf_op jit(solution)/shard_map/ppermute | solution.py:294
  26.5 2.9 %shard_map.50 = (f32[1792,128]{1,0:T(8,128)S(1)}, f32[1792,128]{1,0:T(8,128)S(1)}, bf16[1792,7168]{1,0:T(8,128)(2,1)S(1)}) custom-call(bf16[1920,128]{1,0:T(8,128)(2,1)S(1)} %collective-permute-done.6.first, bf16[1920,128]{1,0:T(8,128)(2,1)S(1)} %collective-permute-done.7.second, ...), custom_call_target="tpu_custom_call", output_to_operand_aliasing={{0}: (3, {}), {1}: (4, {}), {2}: (6, {})} | custom-call | flops 1644167168 | bytes 6422528 | tf_op jit(solution)/shard_map/pallas_call | solution.py:251
  29.4 2.3 %collective-permute-start.9 = (bf16[1920,128]{1,0:T(8,128)(2,1)S(1)}, bf16[1920,128]{1,0:T(8,128)(2,1)S(1)}, u32[]{:S(2)}, u32[]{:S(2)}) collective-permute-start(bf16[1920,128]{1,0:T(8,128)(2,1)S(1)} %collective-permute-done.5.second), channel_id=1, source_target_pairs={{0,4},{1,2},{4,8},{5,1},{8,12},{9,5},{12,15},{13,9},{15,11},{14,13... | collective-permute-start | bytes 1474568 | tf_op jit(solution)/shard_map/ppermute | solution.py:297
  31.7 2.2 %shard_map.51 = (f32[1792,128]{1,0:T(8,128)S(1)}, f32[1792,128]{1,0:T(8,128)S(1)}, bf16[1792,7168]{1,0:T(8,128)(2,1)S(1)}) custom-call(bf16[1920,128]{1,0:T(8,128)(2,1)S(1)} %collective-permute-done.2.first, bf16[1920,128]{1,0:T(8,128)(2,1)S(1)} %collective-permute-done.5.second, ...), custom_call_target="tpu_custom_call", output_to_operand_aliasing={{0}: (3, {}), {1}: (4, {}), {2}: (5, {})} | custom-call | flops 1644167168 | bytes 6422528 | tf_op jit(solution)/shard_map/pallas_call | solution.py:251
  34.6 2.4 %collective-permute-start.8 = (bf16[1920,128]{1,0:T(8,128)(2,1)S(1)}, bf16[1920,128]{1,0:T(8,128)(2,1)S(1)}, u32[]{:S(2)}, u32[]{:S(2)}) collective-permute-start(bf16[1920,128]{1,0:T(8,128)(2,1)S(1)} %collective-permute-done.4.first), channel_id=1, source_target_pairs={{0,4},{1,2},{4,8},{5,1},{8,12},{9,5},{12,15},{13,9},{15,11},{14,13... | collective-permute-start | bytes 1474568 | tf_op jit(solution)/shard_map/ppermute | solution.py:304
  37.0 2.9 %collective-permute-done.9.second = bf16[1920,128]{1,0:T(8,128)(2,1)S(1)} collective-permute-done((bf16[1920,128]{1,0:T(8,128)(2,1)S(1)}, bf16[1920,128]{1,0:T(8,128)(2,1)S(1)}, u32[]{:S(2)}, u32[]{:S(2)}) %collective-permute-start.9) | collective-permute-done | bytes 491552 | tf_op jit(solution)/shard_map/ppermute | solution.py:297
  39.9 5.3 %collective-permute-done.8.first = bf16[1920,128]{1,0:T(8,128)(2,1)S(1)} collective-permute-done((bf16[1920,128]{1,0:T(8,128)(2,1)S(1)}, bf16[1920,128]{1,0:T(8,128)(2,1)S(1)}, u32[]{:S(2)}, u32[]{:S(2)}) %collective-permute-start.8) | collective-permute-done | bytes 491552 | tf_op jit(solution)/shard_map/ppermute | solution.py:304
  47.0 3.3 %collective-permute-start.13 = (f32[1792,128]{1,0:T(8,128)S(1)}, f32[1792,128]{1,0:T(8,128)S(1)}, u32[]{:S(2)}, u32[]{:S(2)}) collective-permute-start(f32[1792,128]{1,0:T(8,128)S(1)} %get-tuple-element.105), channel_id=1, source_target_pairs={{0,1},{1,0},{2,3},{3,2},{4,5},{5,4},{6,7},{7,6},{8,9},{9,8},{10,11... | collective-permute-start | bytes 2752520 | tf_op jit(solution)/shard_map/ppermute | solution.py:21
  56.4 5.1 %collective-permute-done.14.first = bf16[1920,128]{1,0:T(8,128)(2,1)S(1)} collective-permute-done((bf16[1920,128]{1,0:T(8,128)(2,1)S(1)}, bf16[1920,128]{1,0:T(8,128)(2,1)S(1)}, u32[]{:S(2)}, u32[]{:S(2)}) %collective-permute-start.14) | collective-permute-done | bytes 491552 | tf_op jit(solution)/shard_map/ppermute | solution.py:294
  63.6 2.4 %shard_map.56 = (f32[1792,128]{1,0:T(8,128)S(1)}, f32[1792,128]{1,0:T(8,128)S(1)}, bf16[1792,7168]{1,0:T(8,128)(2,1)S(1)}) custom-call(bf16[1920,128]{1,0:T(8,128)(2,1)S(1)} %get-tuple-element.109.first, bf16[1920,128]{1,0:T(8,128)(2,1)S(1)} %collective-permute-done.16.second, ...), custom_call_target="tpu_custom_call", output_to_operand_aliasing={{2}: (3, {})} | custom-call | flops 1644167168 | bytes 6422528 | tf_op jit(solution)/shard_map/pallas_call | solution.py:251
  68.9 2.2 %shard_map.57 = (f32[1792,128]{1,0:T(8,128)S(1)}, f32[1792,128]{1,0:T(8,128)S(1)}, bf16[1792,7168]{1,0:T(8,128)(2,1)S(1)}) custom-call(bf16[1920,128]{1,0:T(8,128)(2,1)S(1)} %collective-permute-done.14.first, bf16[1920,128]{1,0:T(8,128)(2,1)S(1)} %collective-permute-done.17.second, ...), custom_call_target="tpu_custom_call", output_to_operand_aliasing={{0}: (3, {}), {1}: (4, {}), {2}: (5, {})} | custom-call | flops 1644167168 | bytes 6422528 | tf_op jit(solution)/shard_map/pallas_call | solution.py:251
  74.2 2.3 %shard_map.58 = (f32[1792,128]{1,0:T(8,128)S(1)}, f32[1792,128]{1,0:T(8,128)S(1)}, bf16[1792,7168]{1,0:T(8,128)(2,1)S(1)}) custom-call(bf16[1920,128]{1,0:T(8,128)(2,1)S(1)} %collective-permute-done.20.first, bf16[1920,128]{1,0:T(8,128)(2,1)S(1)} %collective-permute-done.21.second, ...), custom_call_target="tpu_custom_call", output_to_operand_aliasing={{0}: (3, {}), {1}: (4, {}), {2}: (5, {})} | custom-call | flops 1644167168 | bytes 6422528 | tf_op jit(solution)/shard_map/pallas_call | solution.py:251
  79.4 2.2 %shard_map.59 = (f32[1792,128]{1,0:T(8,128)S(1)}, f32[1792,128]{1,0:T(8,128)S(1)}, bf16[1792,7168]{1,0:T(8,128)(2,1)S(1)}) custom-call(bf16[1920,128]{1,0:T(8,128)(2,1)S(1)} %collective-permute-done.15.first, bf16[1920,128]{1,0:T(8,128)(2,1)S(1)} %collective-permute-done.19.second, ...), custom_call_target="tpu_custom_call", output_to_operand_aliasing={{0}: (3, {}), {1}: (4, {}), {2}: (5, {})} | custom-call | flops 1644167168 | bytes 6422528 | tf_op jit(solution)/shard_map/pallas_call | solution.py:251
  84.7 3.2 %collective-permute-done.23.second = bf16[1920,128]{1,0:T(8,128)(2,1)S(1)} collective-permute-done((bf16[1920,128]{1,0:T(8,128)(2,1)S(1)}, bf16[1920,128]{1,0:T(8,128)(2,1)S(1)}, u32[]{:S(2)}, u32[]{:S(2)}) %collective-permute-start.23) | collective-permute-done | bytes 491552 | tf_op jit(solution)/shard_map/ppermute | solution.py:297
  87.9 5.3 %collective-permute-done.22.first = bf16[1920,128]{1,0:T(8,128)(2,1)S(1)} collective-permute-done((bf16[1920,128]{1,0:T(8,128)(2,1)S(1)}, bf16[1920,128]{1,0:T(8,128)(2,1)S(1)}, u32[]{:S(2)}, u32[]{:S(2)}) %collective-permute-start.22) | collective-permute-done | bytes 491552 | tf_op jit(solution)/shard_map/ppermute | solution.py:304
  95.0 3.3 %collective-permute-start.27 = (f32[1792,128]{1,0:T(8,128)S(1)}, f32[1792,128]{1,0:T(8,128)S(1)}, u32[]{:S(2)}, u32[]{:S(2)}) collective-permute-start(f32[1792,128]{1,0:T(8,128)S(1)} %get-tuple-element.138), channel_id=1, source_target_pairs={{0,1},{1,0},{2,3},{3,2},{4,5},{5,4},{6,7},{7,6},{8,9},{9,8},{10,11... | collective-permute-start | bytes 2752520 | tf_op jit(solution)/shard_map/ppermute | solution.py:21
  103.8 2.4 %collective-permute-done.29 = f32[8,128]{1,0:T(8,128)S(1)} collective-permute-done((f32[8,128]{1,0:T(8,128)S(1)}, f32[8,128]{1,0:T(8,128)S(1)}, u32[]{:S(2)}, u32[]{:S(2)}) %collective-permute-start.29) | collective-permute-done | bytes 4128 | tf_op jit(solution)/shard_map/ppermute | solution.py:27
  106.3 4.3 %collective-permute-start.33 = (f32[8,128]{1,0:T(8,128)S(1)}, f32[8,128]{1,0:T(8,128)S(1)}, u32[]{:S(2)}, u32[]{:S(2)}) collective-permute-start(f32[8,128]{1,0:T(8,128)S(1)} %add_add_fusion.1), channel_id=1, source_target_pairs={{0,12},{1,13},{2,14},{3,15},{4,0},{5,1},{6,2},{7,3},{8,4},{9,5},{1... | collective-permute-start | bytes 12296 | tf_op jit(solution)/shard_map/ppermute | solution.py:29
  112.0 4.1 %collective-permute-done.31 = f32[8,128]{1,0:T(8,128)S(1)} collective-permute-done((f32[8,128]{1,0:T(8,128)S(1)}, f32[8,128]{1,0:T(8,128)S(1)}, u32[]{:S(2)}, u32[]{:S(2)}) %collective-permute-start.31) | collective-permute-done | bytes 4128 | tf_op jit(solution)/shard_map/ppermute | solution.py:29
  (77 shorter events, 42.8 us)
Async XLA Ops:
  3.9 9.1 %collective-permute-start = (bf16[1920,128]{1,0:T(8,128)(2,1)S(1)}, bf16[1920,128]{1,0:T(8,128)(2,1)S(1)}, u32[]{:S(2)}, u32[]{:S(2)}) collective-permute-start(bf16[1920,128]{1,0:T(8,128)(2,1)S(1)} %shard_map.46.first), channel_id=1, source_target_pairs={{0,4},{1,2},{4,8},{5,1},{8,12},{9,5},{12,15},{13,9},{15,11},{14,13... | collective-permute-start | bytes 1474568 | tf_op jit(solution)/shard_map/ppermute | solution.py:294
  10.5 8.3 %collective-permute-start.3 = (bf16[1920,128]{1,0:T(8,128)(2,1)S(1)}, bf16[1920,128]{1,0:T(8,128)(2,1)S(1)}, u32[]{:S(2)}, u32[]{:S(2)}) collective-permute-start(bf16[1920,128]{1,0:T(8,128)(2,1)S(1)} %get-tuple-element.74.second), channel_id=1, source_target_pairs={{0,4},{1,2},{4,8},{5,1},{8,12},{9,5},{12,15},{13,9},{15,11},{14,13... | collective-permute-start | bytes 1474568 | tf_op jit(solution)/shard_map/ppermute | solution.py:297
  13.0 11.1 %collective-permute-start.2 = (bf16[1920,128]{1,0:T(8,128)(2,1)S(1)}, bf16[1920,128]{1,0:T(8,128)(2,1)S(1)}, u32[]{:S(2)}, u32[]{:S(2)}) collective-permute-start(bf16[1920,128]{1,0:T(8,128)(2,1)S(1)} %collective-permute-done.first), channel_id=1, source_target_pairs={{0,4},{1,2},{4,8},{5,1},{8,12},{9,5},{12,15},{13,9},{15,11},{14,13... | collective-permute-start | bytes 1474568 | tf_op jit(solution)/shard_map/ppermute | solution.py:294
  18.4 8.1 %collective-permute-start.6 = (bf16[1920,128]{1,0:T(8,128)(2,1)S(1)}, bf16[1920,128]{1,0:T(8,128)(2,1)S(1)}, u32[]{:S(2)}, u32[]{:S(2)}) collective-permute-start(bf16[1920,128]{1,0:T(8,128)(2,1)S(1)} %collective-permute-done.first), channel_id=1, source_target_pairs={{0,1},{1,0},{2,3},{3,2},{4,5},{5,4},{6,7},{7,6},{8,9},{9,8},{10,11... | collective-permute-start | bytes 1474568 | tf_op jit(solution)/shard_map/ppermute | solution.py:21
  18.8 7.6 %collective-permute-start.7 = (bf16[1920,128]{1,0:T(8,128)(2,1)S(1)}, bf16[1920,128]{1,0:T(8,128)(2,1)S(1)}, u32[]{:S(2)}, u32[]{:S(2)}) collective-permute-start(bf16[1920,128]{1,0:T(8,128)(2,1)S(1)} %collective-permute-done.3.second), channel_id=1, source_target_pairs={{0,1},{1,0},{2,3},{3,2},{4,5},{5,4},{6,7},{7,6},{8,9},{9,8},{10,11... | collective-permute-start | bytes 1474568 | tf_op jit(solution)/shard_map/ppermute | solution.py:21
  19.0 10.4 %collective-permute-start.5 = (bf16[1920,128]{1,0:T(8,128)(2,1)S(1)}, bf16[1920,128]{1,0:T(8,128)(2,1)S(1)}, u32[]{:S(2)}, u32[]{:S(2)}) collective-permute-start(bf16[1920,128]{1,0:T(8,128)(2,1)S(1)} %collective-permute-done.3.second), channel_id=1, source_target_pairs={{0,4},{1,2},{4,8},{5,1},{8,12},{9,5},{12,15},{13,9},{15,11},{14,13... | collective-permute-start | bytes 1474568 | tf_op jit(solution)/shard_map/ppermute | solution.py:297
  24.1 10.5 %collective-permute-start.4 = (bf16[1920,128]{1,0:T(8,128)(2,1)S(1)}, bf16[1920,128]{1,0:T(8,128)(2,1)S(1)}, u32[]{:S(2)}, u32[]{:S(2)}) collective-permute-start(bf16[1920,128]{1,0:T(8,128)(2,1)S(1)} %collective-permute-done.2.first), channel_id=1, source_target_pairs={{0,4},{1,2},{4,8},{5,1},{8,12},{9,5},{12,15},{13,9},{15,11},{14,13... | collective-permute-start | bytes 1474568 | tf_op jit(solution)/shard_map/ppermute | solution.py:294
  29.4 10.5 %collective-permute-start.9 = (bf16[1920,128]{1,0:T(8,128)(2,1)S(1)}, bf16[1920,128]{1,0:T(8,128)(2,1)S(1)}, u32[]{:S(2)}, u32[]{:S(2)}) collective-permute-start(bf16[1920,128]{1,0:T(8,128)(2,1)S(1)} %collective-permute-done.5.second), channel_id=1, source_target_pairs={{0,4},{1,2},{4,8},{5,1},{8,12},{9,5},{12,15},{13,9},{15,11},{14,13... | collective-permute-start | bytes 1474568 | tf_op jit(solution)/shard_map/ppermute | solution.py:297
  34.6 10.5 %collective-permute-start.8 = (bf16[1920,128]{1,0:T(8,128)(2,1)S(1)}, bf16[1920,128]{1,0:T(8,128)(2,1)S(1)}, u32[]{:S(2)}, u32[]{:S(2)}) collective-permute-start(bf16[1920,128]{1,0:T(8,128)(2,1)S(1)} %collective-permute-done.4.first), channel_id=1, source_target_pairs={{0,4},{1,2},{4,8},{5,1},{8,12},{9,5},{12,15},{13,9},{15,11},{14,13... | collective-permute-start | bytes 1474568 | tf_op jit(solution)/shard_map/ppermute | solution.py:304
  37.0 8.2 %collective-permute-start.11 = (bf16[1920,128]{1,0:T(8,128)(2,1)S(1)}, bf16[1920,128]{1,0:T(8,128)(2,1)S(1)}, u32[]{:S(2)}, u32[]{:S(2)}) collective-permute-start(bf16[1920,128]{1,0:T(8,128)(2,1)S(1)} %collective-permute-done.4.first), channel_id=1, source_target_pairs={{0,1},{1,0},{2,3},{3,2},{4,5},{5,4},{6,7},{7,6},{8,9},{9,8},{10,11... | collective-permute-start | bytes 1474568 | tf_op jit(solution)/shard_map/ppermute | solution.py:21
  53.3 8.3 %collective-permute-start.14 = (bf16[1920,128]{1,0:T(8,128)(2,1)S(1)}, bf16[1920,128]{1,0:T(8,128)(2,1)S(1)}, u32[]{:S(2)}, u32[]{:S(2)}) collective-permute-start(bf16[1920,128]{1,0:T(8,128)(2,1)S(1)} %get-tuple-element.109.first), channel_id=1, source_target_pairs={{0,4},{1,2},{4,8},{5,1},{8,12},{9,5},{12,15},{13,9},{15,11},{14,13... | collective-permute-start | bytes 1474568 | tf_op jit(solution)/shard_map/ppermute | solution.py:294
  54.8 12.0 %collective-permute-start.17 = (bf16[1920,128]{1,0:T(8,128)(2,1)S(1)}, bf16[1920,128]{1,0:T(8,128)(2,1)S(1)}, u32[]{:S(2)}, u32[]{:S(2)}) collective-permute-start(bf16[1920,128]{1,0:T(8,128)(2,1)S(1)} %collective-permute-done.16.second), channel_id=1, source_target_pairs={{0,4},{1,2},{4,8},{5,1},{8,12},{9,5},{12,15},{13,9},{15,11},{14,13... | collective-permute-start | bytes 1474568 | tf_op jit(solution)/shard_map/ppermute | solution.py:297
  61.5 10.5 %collective-permute-start.15 = (bf16[1920,128]{1,0:T(8,128)(2,1)S(1)}, bf16[1920,128]{1,0:T(8,128)(2,1)S(1)}, u32[]{:S(2)}, u32[]{:S(2)}) collective-permute-start(bf16[1920,128]{1,0:T(8,128)(2,1)S(1)} %collective-permute-done.14.first), channel_id=1, source_target_pairs={{0,4},{1,2},{4,8},{5,1},{8,12},{9,5},{12,15},{13,9},{15,11},{14,13... | collective-permute-start | bytes 1474568 | tf_op jit(solution)/shard_map/ppermute | solution.py:294
  66.0 8.1 %collective-permute-start.20 = (bf16[1920,128]{1,0:T(8,128)(2,1)S(1)}, bf16[1920,128]{1,0:T(8,128)(2,1)S(1)}, u32[]{:S(2)}, u32[]{:S(2)}) collective-permute-start(bf16[1920,128]{1,0:T(8,128)(2,1)S(1)} %collective-permute-done.14.first), channel_id=1, source_target_pairs={{0,1},{1,0},{2,3},{3,2},{4,5},{5,4},{6,7},{7,6},{8,9},{9,8},{10,11... | collective-permute-start | bytes 1474568 | tf_op jit(solution)/shard_map/ppermute | solution.py:21
  66.8 7.4 %collective-permute-start.21 = (bf16[1920,128]{1,0:T(8,128)(2,1)S(1)}, bf16[1920,128]{1,0:T(8,128)(2,1)S(1)}, u32[]{:S(2)}, u32[]{:S(2)}) collective-permute-start(bf16[1920,128]{1,0:T(8,128)(2,1)S(1)} %collective-permute-done.17.second), channel_id=1, source_target_pairs={{0,1},{1,0},{2,3},{3,2},{4,5},{5,4},{6,7},{7,6},{8,9},{9,8},{10,11... | collective-permute-start | bytes 1474568 | tf_op jit(solution)/shard_map/ppermute | solution.py:21
  66.8 10.5 %collective-permute-start.19 = (bf16[1920,128]{1,0:T(8,128)(2,1)S(1)}, bf16[1920,128]{1,0:T(8,128)(2,1)S(1)}, u32[]{:S(2)}, u32[]{:S(2)}) collective-permute-start(bf16[1920,128]{1,0:T(8,128)(2,1)S(1)} %collective-permute-done.17.second), channel_id=1, source_target_pairs={{0,4},{1,2},{4,8},{5,1},{8,12},{9,5},{12,15},{13,9},{15,11},{14,13... | collective-permute-start | bytes 1474568 | tf_op jit(solution)/shard_map/ppermute | solution.py:297
  72.1 10.5 %collective-permute-start.18 = (bf16[1920,128]{1,0:T(8,128)(2,1)S(1)}, bf16[1920,128]{1,0:T(8,128)(2,1)S(1)}, u32[]{:S(2)}, u32[]{:S(2)}) collective-permute-start(bf16[1920,128]{1,0:T(8,128)(2,1)S(1)} %collective-permute-done.15.first), channel_id=1, source_target_pairs={{0,4},{1,2},{4,8},{5,1},{8,12},{9,5},{12,15},{13,9},{15,11},{14,13... | collective-permute-start | bytes 1474568 | tf_op jit(solution)/shard_map/ppermute | solution.py:294
  77.3 10.5 %collective-permute-start.23 = (bf16[1920,128]{1,0:T(8,128)(2,1)S(1)}, bf16[1920,128]{1,0:T(8,128)(2,1)S(1)}, u32[]{:S(2)}, u32[]{:S(2)}) collective-permute-start(bf16[1920,128]{1,0:T(8,128)(2,1)S(1)} %collective-permute-done.19.second), channel_id=1, source_target_pairs={{0,4},{1,2},{4,8},{5,1},{8,12},{9,5},{12,15},{13,9},{15,11},{14,13... | collective-permute-start | bytes 1474568 | tf_op jit(solution)/shard_map/ppermute | solution.py:297
  82.6 10.5 %collective-permute-start.22 = (bf16[1920,128]{1,0:T(8,128)(2,1)S(1)}, bf16[1920,128]{1,0:T(8,128)(2,1)S(1)}, u32[]{:S(2)}, u32[]{:S(2)}) collective-permute-start(bf16[1920,128]{1,0:T(8,128)(2,1)S(1)} %collective-permute-done.18.first), channel_id=1, source_target_pairs={{0,4},{1,2},{4,8},{5,1},{8,12},{9,5},{12,15},{13,9},{15,11},{14,13... | collective-permute-start | bytes 1474568 | tf_op jit(solution)/shard_map/ppermute | solution.py:304
  84.7 8.4 %collective-permute-start.25 = (bf16[1920,128]{1,0:T(8,128)(2,1)S(1)}, bf16[1920,128]{1,0:T(8,128)(2,1)S(1)}, u32[]{:S(2)}, u32[]{:S(2)}) collective-permute-start(bf16[1920,128]{1,0:T(8,128)(2,1)S(1)} %collective-permute-done.18.first), channel_id=1, source_target_pairs={{0,1},{1,0},{2,3},{3,2},{4,5},{5,4},{6,7},{7,6},{8,9},{9,8},{10,11... | collective-permute-start | bytes 1474568 | tf_op jit(solution)/shard_map/ppermute | solution.py:21
  95.0 5.4 %collective-permute-start.27 = (f32[1792,128]{1,0:T(8,128)S(1)}, f32[1792,128]{1,0:T(8,128)S(1)}, u32[]{:S(2)}, u32[]{:S(2)}) collective-permute-start(f32[1792,128]{1,0:T(8,128)S(1)} %get-tuple-element.138), channel_id=1, source_target_pairs={{0,1},{1,0},{2,3},{3,2},{4,5},{5,4},{6,7},{7,6},{8,9},{9,8},{10,11... | collective-permute-start | bytes 2752520 | tf_op jit(solution)/shard_map/ppermute | solution.py:21
  106.3 5.7 %collective-permute-start.33 = (f32[8,128]{1,0:T(8,128)S(1)}, f32[8,128]{1,0:T(8,128)S(1)}, u32[]{:S(2)}, u32[]{:S(2)}) collective-permute-start(f32[8,128]{1,0:T(8,128)S(1)} %add_add_fusion.1), channel_id=1, source_target_pairs={{0,12},{1,13},{2,14},{3,15},{4,0},{5,1},{6,2},{7,3},{8,4},{9,5},{1... | collective-permute-start | bytes 12296 | tf_op jit(solution)/shard_map/ppermute | solution.py:29
  110.6 5.4 %collective-permute-start.31 = (f32[8,128]{1,0:T(8,128)S(1)}, f32[8,128]{1,0:T(8,128)S(1)}, u32[]{:S(2)}, u32[]{:S(2)}) collective-permute-start(f32[8,128]{1,0:T(8,128)S(1)} %add_add_fusion.1), channel_id=1, source_target_pairs={{0,4},{1,5},{2,6},{3,7},{4,8},{5,9},{6,10},{7,11},{8,12},{9,13},{1... | collective-permute-start | bytes 12296 | tf_op jit(solution)/shard_map/ppermute | solution.py:29
  110.6 5.4 %collective-permute-start.32 = (f32[8,128]{1,0:T(8,128)S(1)}, f32[8,128]{1,0:T(8,128)S(1)}, u32[]{:S(2)}, u32[]{:S(2)}) collective-permute-start(f32[8,128]{1,0:T(8,128)S(1)} %add_add_fusion.1), channel_id=1, source_target_pairs={{0,8},{1,9},{2,10},{3,11},{4,12},{5,13},{6,14},{7,15},{8,0},{9,1},... | collective-permute-start | bytes 12296 | tf_op jit(solution)/shard_map/ppermute | solution.py:29
  (15 other events, 66.2 us)
where the time goes:
time: 118 us; the launch traced here: 117 us
  starting transfers between devices  44.7 us (38%)
  waiting for transfers between devices  42.8 us (36%)
  Pallas kernels  25.7 us (22%)
  local copies, waits for them, and re-layouts  3.3 us (3%)
    pallas_call x14, Pallas kernels, product(): pl.pallas_call(functools.partial(product_kernel, ring, slot, loads, with_...  20.3 us
    ppermute x6, starting transfers between devices, ring_apply(): came = lax.ppermute(after(first, acc[:1]), AXES, ring.shift())  13 us
    ppermute x6, starting transfers between devices, ring_apply(): second = lax.ppermute(after(second, acc[:1]), AXES, ring.shift())  12.2 us
    ppermute x2, waiting for transfers between devices, ring_apply(): first = lax.ppermute(after(first, acc[:1]), AXES, ring.shift())  10.5 us
    ppermute x6, waiting for transfers between devices, ring_apply(): came = lax.ppermute(after(first, acc[:1]), AXES, ring.shift())  8.29 us
    ppermute x6, waiting for transfers between devices, ring_apply(): second = lax.ppermute(after(second, acc[:1]), AXES, ring.shift())  8.04 us
    ppermute x14, starting transfers between devices, swap(): lax.ppermute(value, axis, [(i, i ^ distance) for i in range(lax.axis_size...  7.84 us
    ppermute x14, waiting for transfers between devices, swap(): lax.ppermute(value, axis, [(i, i ^ distance) for i in range(lax.axis_size...  7.82 us
  transfers between devices with their start and end apart: 34, of which 20 were waited for; matrix products, arithmetic and copies ran while one was open for 0% of the time, Pallas kernels for 20%

commit v1 on v0

--- a/solution.py
+++ b/solution.py
@@ -12,6 +12,7 @@
 PART = 448
 LIMIT = 8 * 1024 * 1024
 AXES = ("row", "col")
+WEIGHTS = ((1, 1, 0.3, 0.3, 8, 0.02, 0.02), (1, 0.02, 0.3, 2, 4, 0.3, 4))
 
 damping_ratio = 0.3
 epsilon = 1e-06
@@ -22,11 +23,12 @@
 
 
 def sum_part(value, count):
-    devices = 2 * count
-    shifts = [[(i, i ^ k) for i in range(devices)] for k in (1, 2, 3)]
-    value += sum(lax.ppermute(value, AXES, pairs) for pairs in shifts)
-    shifts = [[(i, (i + k) % devices) for i in range(devices)] for k in range(4, devices, 4)]
-    return value + sum(lax.ppermute(value, AXES, pairs) for pairs in shifts)
+    value = value + swap(value, "col", 1)
+    distance = 1
+    while distance < count:
+        value = value + swap(value, "row", distance)
+        distance *= 2
+    return value
 
 
 def expand_local(block_mask, row_index, row_block, col_index, width_cols):
@@ -95,16 +97,25 @@
             if self.half(self.source(place, core, step)) != core
         ]
 
+    def close(self, sign):
+        pairs = []
+        for place in range(self.count):
+            core = self.ahead(place - sign)
+            core = core if sign > 0 else 1 - core
+            target = self.half(place + self.count // 2)
+            pairs.append((self.device(place - sign, core), self.device(place, target)))
+        return pairs
+
     def slots(self):
         found = []
         for step in range(self.last):
             found.append((True, step))
             if self.hand_over(step):
                 found.append((False, step))
-        return found + [(True, self.last)]
+        return found
 
     def loads(self, slot):
-        base = 3 * (1 + len(self.slots()))
+        base = 3 * (2 + len(self.slots()))
         return [base + slot + 1] if slot + 1 < self.count // 2 else []
 
     def entry(self, place, core, carrier, step):
@@ -122,6 +133,8 @@
             line = [self.row(place) % half, int(self.half(place) == core), 0]
             for carrier, step in self.slots():
                 line += self.entry(place, core, core if carrier else 1 - core, step)
+            far = place + half
+            line += [self.row(far) % half, int(self.half(far) == core), int(self.ahead(far) != core)]
             needed = [line[k] for k in range(0, len(line), 3) if line[k + 1]]
             line += needed
             lines[self.device(place, core)] = line
@@ -229,6 +242,7 @@
 def product(ring, slot, loads, gram, store, message, across, acts, acc):
     rows = across.shape[0]
     width = message[0].shape[1]
+    weight = WEIGHTS[gram is None][slot]
     whole = pl.BlockSpec(memory_space=pltpu.VMEM)
     with_trace = bool(loads) and slot == 0
     operands = [*message, across]
@@ -257,7 +271,9 @@
         input_output_aliases=aliases,
         compiler_params=pltpu.CompilerParams(vmem_limit_bytes=LIMIT),
         cost_estimate=pl.CostEstimate(
-            flops=4 * rows * rows * width, bytes_accessed=2 * rows * rows, transcendentals=0
+            flops=int(weight * 4 * rows * rows * width),
+            bytes_accessed=int(weight * 2 * rows * rows),
+            transcendentals=0,
         ),
     )(*operands)
     return results[:2], results[2], results[3:]
@@ -301,15 +317,12 @@
         first = came
         held = (first, second)
         ready.append(held)
-    first = lax.ppermute(after(first, acc[:1]), AXES, ring.shift())
+    last = tuple(lax.ppermute(after(first, acc[:1]), AXES, ring.close(sign)) for sign in (1, -1))
     hand_over(ring.last - 1)
-    work()
-    last = (first, swap(after(first, acc[:1]), "col", 1))
     while ready:
         work()
-    ready.append(last)
-    work()
-    return acc[0], swap(acc[1], "col", 1), store, trace
+    (own, other), store, _ = product(ring, slot, [], gram, store, last, across, acts, acc)
+    return own, swap(other, "col", 1), store, trace
 
 
 def put_message(message, acts, rows):

time: 118 us -> 118 us (level)
  starting transfers between devices: 44.7 us -> 62.5 us
  waiting for transfers between devices: 42.8 us -> 25.3 us
    ppermute x14 -> x16, starting transfers between devices: 7.84 us -> 20.2 us  [swap(): lax.ppermute(value, axis, [(i, i ^ distance) for i in range(lax.axis_size...]
    ppermute x8 -> x4, waiting for transfers between devices: 18.6 us -> 7 us  [ring_apply(): lax.ppermute(after(first, acc[:1]), AXES, ring.close(sign))]
    ppermute x6, waiting for transfers between devices: 8.04 us -> 0.52 us  [ring_apply(): second = lax.ppermute(after(second, acc[:1]), AXES, ring.shift())]
    ppermute x14 -> x16, waiting for transfers between devices: 7.82 us -> 13.9 us  [swap(): lax.ppermute(value, axis, [(i, i ^ distance) for i in range(lax.axis_size...]
    ppermute x6, waiting for transfers between devices: 8.29 us -> 3.84 us  [ring_apply(): came = lax.ppermute(after(first, acc[:1]), AXES, ring.shift())]
    ppermute x6, starting transfers between devices: 12.2 us -> 15.9 us  [ring_apply(): second = lax.ppermute(after(second, acc[:1]), AXES, ring.shift())]
    ppermute x6, starting transfers between devices: 13 us -> 15.6 us  [ring_apply(): came = lax.ppermute(after(first, acc[:1]), AXES, ring.shift())]
    ppermute x8 -> x4, starting transfers between devices: 11.7 us -> 10.7 us  [ring_apply(): lax.ppermute(after(first, acc[:1]), AXES, ring.close(sign))]
  transfers between devices with their start and end apart: 34 -> 32, of which waited for: 20 -> 15; matrix products, arithmetic and copies ran while one was open for 0% -> 0% of each run, Pallas kernels for 20% -> 20%
where the time goes in v1:
time: 118 us
  starting transfers between devices  62.5 us (53%)
  Pallas kernels  25.6 us (22%)
  waiting for transfers between devices  25.3 us (21%)
  local copies, waits for them, and re-layouts  3.3 us (3%)
    ppermute x16, starting transfers between devices, swap(): lax.ppermute(value, axis, [(i, i ^ distance) for i in range(lax.axis_size...  20.2 us
    pallas_call x14, Pallas kernels, product(): pl.pallas_call(functools.partial(product_kernel, ring, slot, loads, with_...  20.2 us
    ppermute x6, starting transfers between devices, ring_apply(): second = lax.ppermute(after(second, acc[:1]), AXES, ring.shift())  15.9 us
    ppermute x6, starting transfers between devices, ring_apply(): came = lax.ppermute(after(first, acc[:1]), AXES, ring.shift())  15.6 us
    ppermute x16, waiting for transfers between devices, swap(): lax.ppermute(value, axis, [(i, i ^ distance) for i in range(lax.axis_size...  13.9 us
    ppermute x4, starting transfers between devices, ring_apply(): lax.ppermute(after(first, acc[:1]), AXES, ring.close(sign))  10.7 us
    ppermute x4, waiting for transfers between devices, ring_apply(): lax.ppermute(after(first, acc[:1]), AXES, ring.close(sign))  7 us
    ppermute x6, waiting for transfers between devices, ring_apply(): came = lax.ppermute(after(first, acc[:1]), AXES, ring.shift())  3.84 us
  transfers between devices with their start and end apart: 32, of which 15 were waited for; matrix products, arithmetic and copies ran while one was open for 0% of the time, Pallas kernels for 20%

profile of v1, /device:TPU:0, one launch (start us, length us, event | category | flops | bytes accessed | tf_op | source)
XLA Modules:
  0.0 117.7 jit_solution(2777545945485093701)
XLA Ops:
  3.9 2.6 %collective-permute-start = (bf16[1920,128]{1,0:T(8,128)(2,1)S(1)}, bf16[1920,128]{1,0:T(8,128)(2,1)S(1)}, u32[]{:S(2)}, u32[]{:S(2)}) collective-permute-start(bf16[1920,128]{1,0:T(8,128)(2,1)S(1)} %shard_map.46.first), channel_id=1, source_target_pairs={{0,4},{1,2},{4,8},{5,1},{8,12},{9,5},{12,15},{13,9},{15,11},{14,13... | collective-permute-start | bytes 1474568 | tf_op jit(solution)/shard_map/ppermute | solution.py:310
  7.5 3.0 %shard_map.47 = (bf16[1792,7168]{1,0:T(8,128)(2,1)S(1)}, bf16[1792,128]{1,0:T(8,128)(2,1)S(1)}, bf16[1920,128]{1,0:T(8,128)(2,1)S(1)}) custom-call(bf16[1792,7168]{1,0:T(8,128)(2,1)} %refs_2_.3, bf16[128,1792]{1,0:T(8,128)(2,1)S(1)} %copy-done.1, bf16[1920,128]{1,0:T(8,128)(2,1)S(1)} %collective-permute-done.1.second), custom_call_target="tpu_custom_call", output_to_operand_aliasing={{2}: (2, {})} | custom-call | tf_op jit(solution)/shard_map/pallas_call | solution.py:175
  13.0 2.4 %collective-permute-start.2 = (bf16[1920,128]{1,0:T(8,128)(2,1)S(1)}, bf16[1920,128]{1,0:T(8,128)(2,1)S(1)}, u32[]{:S(2)}, u32[]{:S(2)}) collective-permute-start(bf16[1920,128]{1,0:T(8,128)(2,1)S(1)} %collective-permute-done.first), channel_id=1, source_target_pairs={{0,4},{1,2},{4,8},{5,1},{8,12},{9,5},{12,15},{13,9},{15,11},{14,13... | collective-permute-start | bytes 1474568 | tf_op jit(solution)/shard_map/ppermute | solution.py:310
  15.4 3.0 %shard_map.48 = (f32[1792,128]{1,0:T(8,128)S(1)}, f32[1792,128]{1,0:T(8,128)S(1)}, bf16[1792,7168]{1,0:T(8,128)(2,1)S(1)}, f32[8,128]{1,0:T(8,128)S(1)}) custom-call(bf16[1920,128]{1,0:T(8,128)(2,1)S(1)} %shard_map.46.first, bf16[1920,128]{1,0:T(8,128)(2,1)S(1)} %get-tuple-element.72.second, ...), custom_call_target="tpu_custom_call", output_to_operand_aliasing={{2}: (5, {})} | custom-call | flops 1644167168 | bytes 6422528 | tf_op jit(solution)/shard_map/pallas_call | solution.py:265
  21.2 2.9 %shard_map.49 = (f32[1792,128]{1,0:T(8,128)S(1)}, f32[1792,128]{1,0:T(8,128)S(1)}, bf16[1792,7168]{1,0:T(8,128)(2,1)S(1)}) custom-call(bf16[1920,128]{1,0:T(8,128)(2,1)S(1)} %collective-permute-done.first, bf16[1920,128]{1,0:T(8,128)(2,1)S(1)} %collective-permute-done.3.second, ...), custom_call_target="tpu_custom_call", output_to_operand_aliasing={{0}: (3, {}), {1}: (4, {}), {2}: (6, {})} | custom-call | flops 1644167168 | bytes 6422528 | tf_op jit(solution)/shard_map/pallas_call | solution.py:265
  24.1 2.3 %collective-permute-start.4 = (bf16[1920,128]{1,0:T(8,128)(2,1)S(1)}, bf16[1920,128]{1,0:T(8,128)(2,1)S(1)}, u32[]{:S(2)}, u32[]{:S(2)}) collective-permute-start(bf16[1920,128]{1,0:T(8,128)(2,1)S(1)} %collective-permute-done.2.first), channel_id=1, source_target_pairs={{0,4},{1,2},{4,8},{5,1},{8,12},{9,5},{12,15},{13,9},{15,11},{14,13... | collective-permute-start | bytes 1474568 | tf_op jit(solution)/shard_map/ppermute | solution.py:310
  26.5 2.9 %shard_map.50 = (f32[1792,128]{1,0:T(8,128)S(1)}, f32[1792,128]{1,0:T(8,128)S(1)}, bf16[1792,7168]{1,0:T(8,128)(2,1)S(1)}) custom-call(bf16[1920,128]{1,0:T(8,128)(2,1)S(1)} %collective-permute-done.6.first, bf16[1920,128]{1,0:T(8,128)(2,1)S(1)} %collective-permute-done.7.second, ...), custom_call_target="tpu_custom_call", output_to_operand_aliasing={{0}: (3, {}), {1}: (4, {}), {2}: (6, {})} | custom-call | flops 493250144 | bytes 1926758 | tf_op jit(solution)/shard_map/pallas_call | solution.py:265
  29.4 2.3 %collective-permute-start.11 = (bf16[1920,128]{1,0:T(8,128)(2,1)S(1)}, bf16[1920,128]{1,0:T(8,128)(2,1)S(1)}, u32[]{:S(2)}, u32[]{:S(2)}) collective-permute-start(bf16[1920,128]{1,0:T(8,128)(2,1)S(1)} %collective-permute-done.5.second), channel_id=1, source_target_pairs={{0,4},{1,2},{4,8},{5,1},{8,12},{9,5},{12,15},{13,9},{15,11},{14,13... | collective-permute-start | bytes 1474568 | tf_op jit(solution)/shard_map/ppermute | solution.py:313
  34.6 4.4 %collective-permute-start.8 = (bf16[1920,128]{1,0:T(8,128)(2,1)S(1)}, bf16[1920,128]{1,0:T(8,128)(2,1)S(1)}, u32[]{:S(2)}, u32[]{:S(2)}) collective-permute-start(bf16[1920,128]{1,0:T(8,128)(2,1)S(1)} %collective-permute-done.4.first), channel_id=1, source_target_pairs={{3,1},{0,5},{4,8},{8,12},{12,14},{15,10},{11,7},{7,3},{19,17},{16,... | collective-permute-start | bytes 1474568 | tf_op jit(solution)/shard_map/ppermute | solution.py:320
  42.0 3.3 %collective-permute-done.8.first = bf16[1920,128]{1,0:T(8,128)(2,1)S(1)} collective-permute-done((bf16[1920,128]{1,0:T(8,128)(2,1)S(1)}, bf16[1920,128]{1,0:T(8,128)(2,1)S(1)}, u32[]{:S(2)}, u32[]{:S(2)}) %collective-permute-start.8) | collective-permute-done | bytes 491552 | tf_op jit(solution)/shard_map/ppermute | solution.py:320
  45.3 3.6 %collective-permute-start.13 = (f32[1792,128]{1,0:T(8,128)S(1)}, f32[1792,128]{1,0:T(8,128)S(1)}, u32[]{:S(2)}, u32[]{:S(2)}) collective-permute-start(f32[1792,128]{1,0:T(8,128)S(1)} %get-tuple-element.102), channel_id=1, source_target_pairs={{0,1},{1,0},{2,3},{3,2},{4,5},{5,4},{6,7},{7,6},{8,9},{9,8},{10,11... | collective-permute-start | bytes 2752520 | tf_op jit(solution)/shard_map/ppermute | solution.py:22
  53.6 4.0 %collective-permute-start.17 = (bf16[1920,128]{1,0:T(8,128)(2,1)S(1)}, bf16[1920,128]{1,0:T(8,128)(2,1)S(1)}, u32[]{:S(2)}, u32[]{:S(2)}) collective-permute-start(bf16[1920,128]{1,0:T(8,128)(2,1)S(1)} %collective-permute-done.16.second), channel_id=1, source_target_pairs={{0,4},{1,2},{4,8},{5,1},{8,12},{9,5},{12,15},{13,9},{15,11},{14,13... | collective-permute-start | bytes 1474568 | tf_op jit(solution)/shard_map/ppermute | solution.py:313
  57.6 2.5 %collective-permute-done.14.first = bf16[1920,128]{1,0:T(8,128)(2,1)S(1)} collective-permute-done((bf16[1920,128]{1,0:T(8,128)(2,1)S(1)}, bf16[1920,128]{1,0:T(8,128)(2,1)S(1)}, u32[]{:S(2)}, u32[]{:S(2)}) %collective-permute-start.14) | collective-permute-done | bytes 491552 | tf_op jit(solution)/shard_map/ppermute | solution.py:310
  60.2 3.8 %collective-permute-start.15 = (bf16[1920,128]{1,0:T(8,128)(2,1)S(1)}, bf16[1920,128]{1,0:T(8,128)(2,1)S(1)}, u32[]{:S(2)}, u32[]{:S(2)}) collective-permute-start(bf16[1920,128]{1,0:T(8,128)(2,1)S(1)} %collective-permute-done.14.first), channel_id=1, source_target_pairs={{0,4},{1,2},{4,8},{5,1},{8,12},{9,5},{12,15},{13,9},{15,11},{14,13... | collective-permute-start | bytes 1474568 | tf_op jit(solution)/shard_map/ppermute | solution.py:310
  64.0 2.4 %shard_map.56 = (f32[1792,128]{1,0:T(8,128)S(1)}, f32[1792,128]{1,0:T(8,128)S(1)}, bf16[1792,7168]{1,0:T(8,128)(2,1)S(1)}) custom-call(bf16[1920,128]{1,0:T(8,128)(2,1)S(1)} %get-tuple-element.106.first, bf16[1920,128]{1,0:T(8,128)(2,1)S(1)} %collective-permute-done.16.second, ...), custom_call_target="tpu_custom_call", output_to_operand_aliasing={{2}: (3, {})} | custom-call | flops 1644167168 | bytes 6422528 | tf_op jit(solution)/shard_map/pallas_call | solution.py:265
  66.9 2.6 %collective-permute-start.19 = (bf16[1920,128]{1,0:T(8,128)(2,1)S(1)}, bf16[1920,128]{1,0:T(8,128)(2,1)S(1)}, u32[]{:S(2)}, u32[]{:S(2)}) collective-permute-start(bf16[1920,128]{1,0:T(8,128)(2,1)S(1)} %collective-permute-done.17.second), channel_id=1, source_target_pairs={{0,4},{1,2},{4,8},{5,1},{8,12},{9,5},{12,15},{13,9},{15,11},{14,13... | collective-permute-start | bytes 1474568 | tf_op jit(solution)/shard_map/ppermute | solution.py:313
  71.7 2.8 %collective-permute-start.18 = (bf16[1920,128]{1,0:T(8,128)(2,1)S(1)}, bf16[1920,128]{1,0:T(8,128)(2,1)S(1)}, u32[]{:S(2)}, u32[]{:S(2)}) collective-permute-start(bf16[1920,128]{1,0:T(8,128)(2,1)S(1)} %collective-permute-done.15.first), channel_id=1, source_target_pairs={{0,4},{1,2},{4,8},{5,1},{8,12},{9,5},{12,15},{13,9},{15,11},{14,13... | collective-permute-start | bytes 1474568 | tf_op jit(solution)/shard_map/ppermute | solution.py:310
  74.5 2.3 %shard_map.58 = (f32[1792,128]{1,0:T(8,128)S(1)}, f32[1792,128]{1,0:T(8,128)S(1)}, bf16[1792,7168]{1,0:T(8,128)(2,1)S(1)}) custom-call(bf16[1920,128]{1,0:T(8,128)(2,1)S(1)} %collective-permute-done.20.first, bf16[1920,128]{1,0:T(8,128)(2,1)S(1)} %collective-permute-done.21.second, ...), custom_call_target="tpu_custom_call", output_to_operand_aliasing={{0}: (3, {}), {1}: (4, {}), {2}: (5, {})} | custom-call | flops 493250144 | bytes 1926758 | tf_op jit(solution)/shard_map/pallas_call | solution.py:265
  76.8 3.0 %collective-permute-start.25 = (bf16[1920,128]{1,0:T(8,128)(2,1)S(1)}, bf16[1920,128]{1,0:T(8,128)(2,1)S(1)}, u32[]{:S(2)}, u32[]{:S(2)}) collective-permute-start(bf16[1920,128]{1,0:T(8,128)(2,1)S(1)} %collective-permute-done.19.second), channel_id=1, source_target_pairs={{0,4},{1,2},{4,8},{5,1},{8,12},{9,5},{12,15},{13,9},{15,11},{14,13... | collective-permute-start | bytes 1474568 | tf_op jit(solution)/shard_map/ppermute | solution.py:313
  82.1 5.0 %collective-permute-start.22 = (bf16[1920,128]{1,0:T(8,128)(2,1)S(1)}, bf16[1920,128]{1,0:T(8,128)(2,1)S(1)}, u32[]{:S(2)}, u32[]{:S(2)}) collective-permute-start(bf16[1920,128]{1,0:T(8,128)(2,1)S(1)} %collective-permute-done.18.first), channel_id=1, source_target_pairs={{3,1},{0,5},{4,8},{8,12},{12,14},{15,10},{11,7},{7,3},{19,17},{16,... | collective-permute-start | bytes 1474568 | tf_op jit(solution)/shard_map/ppermute | solution.py:320
  89.7 3.7 %collective-permute-done.22.first = bf16[1920,128]{1,0:T(8,128)(2,1)S(1)} collective-permute-done((bf16[1920,128]{1,0:T(8,128)(2,1)S(1)}, bf16[1920,128]{1,0:T(8,128)(2,1)S(1)}, u32[]{:S(2)}, u32[]{:S(2)}) %collective-permute-start.22) | collective-permute-done | bytes 491552 | tf_op jit(solution)/shard_map/ppermute | solution.py:320
  93.4 3.6 %collective-permute-start.27 = (f32[1792,128]{1,0:T(8,128)S(1)}, f32[1792,128]{1,0:T(8,128)S(1)}, u32[]{:S(2)}, u32[]{:S(2)}) collective-permute-start(f32[1792,128]{1,0:T(8,128)S(1)} %get-tuple-element.134), channel_id=1, source_target_pairs={{0,1},{1,0},{2,3},{3,2},{4,5},{5,4},{6,7},{7,6},{8,9},{9,8},{10,11... | collective-permute-start | bytes 2752520 | tf_op jit(solution)/shard_map/ppermute | solution.py:22
  101.8 2.4 %collective-permute-done.29 = f32[8,128]{1,0:T(8,128)S(1)} collective-permute-done((f32[8,128]{1,0:T(8,128)S(1)}, f32[8,128]{1,0:T(8,128)S(1)}, u32[]{:S(2)}, u32[]{:S(2)}) %collective-permute-start.29) | collective-permute-done | bytes 4128 | tf_op jit(solution)/shard_map/ppermute | solution.py:22
  108.0 6.7 %collective-permute-start.31 = (f32[8,128]{1,0:T(8,128)S(1)}, f32[8,128]{1,0:T(8,128)S(1)}, u32[]{:S(2)}, u32[]{:S(2)}) collective-permute-start(f32[8,128]{1,0:T(8,128)S(1)} %add.22), channel_id=1, source_target_pairs={{0,8},{2,10},{4,12},{6,14},{8,0},{10,2},{12,4},{14,6},{1,9},{3,11}... | collective-permute-start | bytes 12296 | tf_op jit(solution)/shard_map/ppermute | solution.py:22
  (75 shorter events, 40.0 us)
Async XLA Ops:
  3.9 9.1 %collective-permute-start = (bf16[1920,128]{1,0:T(8,128)(2,1)S(1)}, bf16[1920,128]{1,0:T(8,128)(2,1)S(1)}, u32[]{:S(2)}, u32[]{:S(2)}) collective-permute-start(bf16[1920,128]{1,0:T(8,128)(2,1)S(1)} %shard_map.46.first), channel_id=1, source_target_pairs={{0,4},{1,2},{4,8},{5,1},{8,12},{9,5},{12,15},{13,9},{15,11},{14,13... | collective-permute-start | bytes 1474568 | tf_op jit(solution)/shard_map/ppermute | solution.py:310
  10.5 8.3 %collective-permute-start.3 = (bf16[1920,128]{1,0:T(8,128)(2,1)S(1)}, bf16[1920,128]{1,0:T(8,128)(2,1)S(1)}, u32[]{:S(2)}, u32[]{:S(2)}) collective-permute-start(bf16[1920,128]{1,0:T(8,128)(2,1)S(1)} %get-tuple-element.72.second), channel_id=1, source_target_pairs={{0,4},{1,2},{4,8},{5,1},{8,12},{9,5},{12,15},{13,9},{15,11},{14,13... | collective-permute-start | bytes 1474568 | tf_op jit(solution)/shard_map/ppermute | solution.py:313
  13.0 11.1 %collective-permute-start.2 = (bf16[1920,128]{1,0:T(8,128)(2,1)S(1)}, bf16[1920,128]{1,0:T(8,128)(2,1)S(1)}, u32[]{:S(2)}, u32[]{:S(2)}) collective-permute-start(bf16[1920,128]{1,0:T(8,128)(2,1)S(1)} %collective-permute-done.first), channel_id=1, source_target_pairs={{0,4},{1,2},{4,8},{5,1},{8,12},{9,5},{12,15},{13,9},{15,11},{14,13... | collective-permute-start | bytes 1474568 | tf_op jit(solution)/shard_map/ppermute | solution.py:310
  18.4 5.7 %collective-permute-start.6 = (bf16[1920,128]{1,0:T(8,128)(2,1)S(1)}, bf16[1920,128]{1,0:T(8,128)(2,1)S(1)}, u32[]{:S(2)}, u32[]{:S(2)}) collective-permute-start(bf16[1920,128]{1,0:T(8,128)(2,1)S(1)} %collective-permute-done.first), channel_id=1, source_target_pairs={{0,1},{1,0},{2,3},{3,2},{4,5},{5,4},{6,7},{7,6},{8,9},{9,8},{10,11... | collective-permute-start | bytes 1474568 | tf_op jit(solution)/shard_map/ppermute | solution.py:22
  18.8 7.6 %collective-permute-start.7 = (bf16[1920,128]{1,0:T(8,128)(2,1)S(1)}, bf16[1920,128]{1,0:T(8,128)(2,1)S(1)}, u32[]{:S(2)}, u32[]{:S(2)}) collective-permute-start(bf16[1920,128]{1,0:T(8,128)(2,1)S(1)} %collective-permute-done.3.second), channel_id=1, source_target_pairs={{0,1},{1,0},{2,3},{3,2},{4,5},{5,4},{6,7},{7,6},{8,9},{9,8},{10,11... | collective-permute-start | bytes 1474568 | tf_op jit(solution)/shard_map/ppermute | solution.py:22
  19.0 10.4 %collective-permute-start.5 = (bf16[1920,128]{1,0:T(8,128)(2,1)S(1)}, bf16[1920,128]{1,0:T(8,128)(2,1)S(1)}, u32[]{:S(2)}, u32[]{:S(2)}) collective-permute-start(bf16[1920,128]{1,0:T(8,128)(2,1)S(1)} %collective-permute-done.3.second), channel_id=1, source_target_pairs={{0,4},{1,2},{4,8},{5,1},{8,12},{9,5},{12,15},{13,9},{15,11},{14,13... | collective-permute-start | bytes 1474568 | tf_op jit(solution)/shard_map/ppermute | solution.py:313
  24.1 10.5 %collective-permute-start.4 = (bf16[1920,128]{1,0:T(8,128)(2,1)S(1)}, bf16[1920,128]{1,0:T(8,128)(2,1)S(1)}, u32[]{:S(2)}, u32[]{:S(2)}) collective-permute-start(bf16[1920,128]{1,0:T(8,128)(2,1)S(1)} %collective-permute-done.2.first), channel_id=1, source_target_pairs={{0,4},{1,2},{4,8},{5,1},{8,12},{9,5},{12,15},{13,9},{15,11},{14,13... | collective-permute-start | bytes 1474568 | tf_op jit(solution)/shard_map/ppermute | solution.py:310
  29.4 10.5 %collective-permute-start.11 = (bf16[1920,128]{1,0:T(8,128)(2,1)S(1)}, bf16[1920,128]{1,0:T(8,128)(2,1)S(1)}, u32[]{:S(2)}, u32[]{:S(2)}) collective-permute-start(bf16[1920,128]{1,0:T(8,128)(2,1)S(1)} %collective-permute-done.5.second), channel_id=1, source_target_pairs={{0,4},{1,2},{4,8},{5,1},{8,12},{9,5},{12,15},{13,9},{15,11},{14,13... | collective-permute-start | bytes 1474568 | tf_op jit(solution)/shard_map/ppermute | solution.py:313
  34.6 5.9 %collective-permute-start.10 = (bf16[1920,128]{1,0:T(8,128)(2,1)S(1)}, bf16[1920,128]{1,0:T(8,128)(2,1)S(1)}, u32[]{:S(2)}, u32[]{:S(2)}) collective-permute-start(bf16[1920,128]{1,0:T(8,128)(2,1)S(1)} %collective-permute-done.4.first), channel_id=1, source_target_pairs={{0,1},{1,0},{2,3},{3,2},{4,5},{5,4},{6,7},{7,6},{8,9},{9,8},{10,11... | collective-permute-start | bytes 1474568 | tf_op jit(solution)/shard_map/ppermute | solution.py:22
  34.6 10.7 %collective-permute-start.8 = (bf16[1920,128]{1,0:T(8,128)(2,1)S(1)}, bf16[1920,128]{1,0:T(8,128)(2,1)S(1)}, u32[]{:S(2)}, u32[]{:S(2)}) collective-permute-start(bf16[1920,128]{1,0:T(8,128)(2,1)S(1)} %collective-permute-done.4.first), channel_id=1, source_target_pairs={{3,1},{0,5},{4,8},{8,12},{12,14},{15,10},{11,7},{7,3},{19,17},{16,... | collective-permute-start | bytes 1474568 | tf_op jit(solution)/shard_map/ppermute | solution.py:320
  39.0 6.3 %collective-permute-start.9 = (bf16[1920,128]{1,0:T(8,128)(2,1)S(1)}, bf16[1920,128]{1,0:T(8,128)(2,1)S(1)}, u32[]{:S(2)}, u32[]{:S(2)}) collective-permute-start(bf16[1920,128]{1,0:T(8,128)(2,1)S(1)} %collective-permute-done.4.first), channel_id=1, source_target_pairs={{5,1},{9,5},{13,8},{14,12},{10,14},{6,10},{2,7},{1,3},{21,17},{25,... | collective-permute-start | bytes 1474568 | tf_op jit(solution)/shard_map/ppermute | solution.py:320
  51.9 8.3 %collective-permute-start.14 = (bf16[1920,128]{1,0:T(8,128)(2,1)S(1)}, bf16[1920,128]{1,0:T(8,128)(2,1)S(1)}, u32[]{:S(2)}, u32[]{:S(2)}) collective-permute-start(bf16[1920,128]{1,0:T(8,128)(2,1)S(1)} %get-tuple-element.106.first), channel_id=1, source_target_pairs={{0,4},{1,2},{4,8},{5,1},{8,12},{9,5},{12,15},{13,9},{15,11},{14,13... | collective-permute-start | bytes 1474568 | tf_op jit(solution)/shard_map/ppermute | solution.py:310
  53.6 12.8 %collective-permute-start.17 = (bf16[1920,128]{1,0:T(8,128)(2,1)S(1)}, bf16[1920,128]{1,0:T(8,128)(2,1)S(1)}, u32[]{:S(2)}, u32[]{:S(2)}) collective-permute-start(bf16[1920,128]{1,0:T(8,128)(2,1)S(1)} %collective-permute-done.16.second), channel_id=1, source_target_pairs={{0,4},{1,2},{4,8},{5,1},{8,12},{9,5},{12,15},{13,9},{15,11},{14,13... | collective-permute-start | bytes 1474568 | tf_op jit(solution)/shard_map/ppermute | solution.py:313
  60.2 11.6 %collective-permute-start.15 = (bf16[1920,128]{1,0:T(8,128)(2,1)S(1)}, bf16[1920,128]{1,0:T(8,128)(2,1)S(1)}, u32[]{:S(2)}, u32[]{:S(2)}) collective-permute-start(bf16[1920,128]{1,0:T(8,128)(2,1)S(1)} %collective-permute-done.14.first), channel_id=1, source_target_pairs={{0,4},{1,2},{4,8},{5,1},{8,12},{9,5},{12,15},{13,9},{15,11},{14,13... | collective-permute-start | bytes 1474568 | tf_op jit(solution)/shard_map/ppermute | solution.py:310
  66.3 8.1 %collective-permute-start.20 = (bf16[1920,128]{1,0:T(8,128)(2,1)S(1)}, bf16[1920,128]{1,0:T(8,128)(2,1)S(1)}, u32[]{:S(2)}, u32[]{:S(2)}) collective-permute-start(bf16[1920,128]{1,0:T(8,128)(2,1)S(1)} %collective-permute-done.14.first), channel_id=1, source_target_pairs={{0,1},{1,0},{2,3},{3,2},{4,5},{5,4},{6,7},{7,6},{8,9},{9,8},{10,11... | collective-permute-start | bytes 1474568 | tf_op jit(solution)/shard_map/ppermute | solution.py:22
  66.4 8.1 %collective-permute-start.21 = (bf16[1920,128]{1,0:T(8,128)(2,1)S(1)}, bf16[1920,128]{1,0:T(8,128)(2,1)S(1)}, u32[]{:S(2)}, u32[]{:S(2)}) collective-permute-start(bf16[1920,128]{1,0:T(8,128)(2,1)S(1)} %collective-permute-done.17.second), channel_id=1, source_target_pairs={{0,1},{1,0},{2,3},{3,2},{4,5},{5,4},{6,7},{7,6},{8,9},{9,8},{10,11... | collective-permute-start | bytes 1474568 | tf_op jit(solution)/shard_map/ppermute | solution.py:22
  66.9 9.8 %collective-permute-start.19 = (bf16[1920,128]{1,0:T(8,128)(2,1)S(1)}, bf16[1920,128]{1,0:T(8,128)(2,1)S(1)}, u32[]{:S(2)}, u32[]{:S(2)}) collective-permute-start(bf16[1920,128]{1,0:T(8,128)(2,1)S(1)} %collective-permute-done.17.second), channel_id=1, source_target_pairs={{0,4},{1,2},{4,8},{5,1},{8,12},{9,5},{12,15},{13,9},{15,11},{14,13... | collective-permute-start | bytes 1474568 | tf_op jit(solution)/shard_map/ppermute | solution.py:313
  71.7 10.3 %collective-permute-start.18 = (bf16[1920,128]{1,0:T(8,128)(2,1)S(1)}, bf16[1920,128]{1,0:T(8,128)(2,1)S(1)}, u32[]{:S(2)}, u32[]{:S(2)}) collective-permute-start(bf16[1920,128]{1,0:T(8,128)(2,1)S(1)} %collective-permute-done.15.first), channel_id=1, source_target_pairs={{0,4},{1,2},{4,8},{5,1},{8,12},{9,5},{12,15},{13,9},{15,11},{14,13... | collective-permute-start | bytes 1474568 | tf_op jit(solution)/shard_map/ppermute | solution.py:310
  76.8 11.0 %collective-permute-start.25 = (bf16[1920,128]{1,0:T(8,128)(2,1)S(1)}, bf16[1920,128]{1,0:T(8,128)(2,1)S(1)}, u32[]{:S(2)}, u32[]{:S(2)}) collective-permute-start(bf16[1920,128]{1,0:T(8,128)(2,1)S(1)} %collective-permute-done.19.second), channel_id=1, source_target_pairs={{0,4},{1,2},{4,8},{5,1},{8,12},{9,5},{12,15},{13,9},{15,11},{14,13... | collective-permute-start | bytes 1474568 | tf_op jit(solution)/shard_map/ppermute | solution.py:313
  82.0 5.9 %collective-permute-start.24 = (bf16[1920,128]{1,0:T(8,128)(2,1)S(1)}, bf16[1920,128]{1,0:T(8,128)(2,1)S(1)}, u32[]{:S(2)}, u32[]{:S(2)}) collective-permute-start(bf16[1920,128]{1,0:T(8,128)(2,1)S(1)} %collective-permute-done.18.first), channel_id=1, source_target_pairs={{0,1},{1,0},{2,3},{3,2},{4,5},{5,4},{6,7},{7,6},{8,9},{9,8},{10,11... | collective-permute-start | bytes 1474568 | tf_op jit(solution)/shard_map/ppermute | solution.py:22
  82.1 11.3 %collective-permute-start.22 = (bf16[1920,128]{1,0:T(8,128)(2,1)S(1)}, bf16[1920,128]{1,0:T(8,128)(2,1)S(1)}, u32[]{:S(2)}, u32[]{:S(2)}) collective-permute-start(bf16[1920,128]{1,0:T(8,128)(2,1)S(1)} %collective-permute-done.18.first), channel_id=1, source_target_pairs={{3,1},{0,5},{4,8},{8,12},{12,14},{15,10},{11,7},{7,3},{19,17},{16,... | collective-permute-start | bytes 1474568 | tf_op jit(solution)/shard_map/ppermute | solution.py:320
  87.1 6.3 %collective-permute-start.23 = (bf16[1920,128]{1,0:T(8,128)(2,1)S(1)}, bf16[1920,128]{1,0:T(8,128)(2,1)S(1)}, u32[]{:S(2)}, u32[]{:S(2)}) collective-permute-start(bf16[1920,128]{1,0:T(8,128)(2,1)S(1)} %collective-permute-done.18.first), channel_id=1, source_target_pairs={{5,1},{9,5},{13,8},{14,12},{10,14},{6,10},{2,7},{1,3},{21,17},{25,... | collective-permute-start | bytes 1474568 | tf_op jit(solution)/shard_map/ppermute | solution.py:320
  93.4 5.7 %collective-permute-start.27 = (f32[1792,128]{1,0:T(8,128)S(1)}, f32[1792,128]{1,0:T(8,128)S(1)}, u32[]{:S(2)}, u32[]{:S(2)}) collective-permute-start(f32[1792,128]{1,0:T(8,128)S(1)} %get-tuple-element.134), channel_id=1, source_target_pairs={{0,1},{1,0},{2,3},{3,2},{4,5},{5,4},{6,7},{7,6},{8,9},{9,8},{10,11... | collective-permute-start | bytes 2752520 | tf_op jit(solution)/shard_map/ppermute | solution.py:22
  108.0 8.3 %collective-permute-start.31 = (f32[8,128]{1,0:T(8,128)S(1)}, f32[8,128]{1,0:T(8,128)S(1)}, u32[]{:S(2)}, u32[]{:S(2)}) collective-permute-start(f32[8,128]{1,0:T(8,128)S(1)} %add.22), channel_id=1, source_target_pairs={{0,8},{2,10},{4,12},{6,14},{8,0},{10,2},{12,4},{14,6},{1,9},{3,11}... | collective-permute-start | bytes 12296 | tf_op jit(solution)/shard_map/ppermute | solution.py:22
  (13 other events, 62.6 us)
